TPU v7x, 32 devices: a whole 2x2x4 slice. The times are simulated.
32 devices in a mesh: neuron: 4 (over z), tm: 2 (over core), trial: 4 (over y, x).
Axes of the slice: x: 2, y: 2, z: 4, core: 2. Of those that a mesh axis runs over, the one named last changes fastest.
Arguments:
- tensor: bfloat16 [1024, 256, 512], P('neuron', 'tm', 'trial'), may hold values from -6 to 6
- present_blocks: int32 [8, 16], P('neuron'), may hold values 0 or 1
- trial_day: int32 [512], P('trial'), may hold values from 0 to 15
- time_factor: bfloat16 [256, 256], P('tm'), may hold values from 0 to 1
- trial_factor: bfloat16 [512, 256], P('trial'), may hold values from 0 to 1
Outputs:
- neuron_out: bfloat16 [1024, 256], P(('neuron', 'tm', 'trial'))
- time_out: bfloat16 [256, 256], P('tm')
- trial_out: bfloat16 [512, 256], P('trial')
All inputs are finite; a program needn't handle non-finite values. No bound on the sum of `present_blocks` on one device may be relied on, other than what follows from the above.
Results may differ from a plain program's by a relative error of at most 0.0051.
The roundings to bfloat16 on the way count: a program that leaves them out, or rounds other values in their place, can miss the bound.
Values may be sent and summed in bfloat16 or wider, within the bound.
A program may use at most 128 MiB of HBM per device.

v0:
```python
import jax
import jax.numpy as jnp
from jax import lax
from jax.sharding import PartitionSpec as P

RIDGE = 0.1
EPSILON = 1e-06


def normal_inverse(gram_matrix):
    order_size = gram_matrix.shape[0]
    identity = jnp.eye(order_size, dtype=jnp.float32)
    scaled = gram_matrix / jnp.mean(jnp.diagonal(gram_matrix)) + RIDGE * identity
    lower_factor = jnp.linalg.cholesky(scaled)
    return jax.scipy.linalg.cho_solve((lower_factor, True), identity)


def apply_inverse(partial_sums, inverse):
    return jnp.dot(partial_sums, inverse, precision=lax.Precision.HIGHEST)


def raw_gram(raw_rows):
    return jnp.dot(raw_rows.T, raw_rows, precision=lax.Precision.HIGHEST)


def khatri_rao(left_rows, right_rows):
    return (
        left_rows.astype(jnp.float32)[:, None, :] * right_rows.astype(jnp.float32)[None, :, :]
    ).astype(jnp.bfloat16)


def rescale(raw_rows, gram_sum, total_rows):
    scales = jnp.sqrt(jnp.diagonal(gram_sum) / total_rows + EPSILON)
    factor = (raw_rows / scales[None, :]).astype(jnp.bfloat16)
    normed = gram_sum / (scales[:, None] * scales[None, :])
    return (factor, normed)


def mask_tensor(tensor, present_blocks, trial_day):
    day_count = present_blocks.shape[1]
    onehot = (trial_day[:, None] == jnp.arange(day_count, dtype=jnp.int32)[None, :]).astype(
        jnp.float32
    )
    block_mask = jnp.dot(present_blocks.astype(jnp.float32), onehot.T)
    block_count = present_blocks.shape[0]
    shaped = tensor.reshape(
        block_count, tensor.shape[0] // block_count, tensor.shape[1], tensor.shape[2]
    )
    return shaped * block_mask.astype(jnp.bfloat16)[:, None, None, :]


def on_device(tensor, present_blocks, trial_day, time_factor, trial_factor):
    blocks = mask_tensor(tensor, present_blocks, trial_day)
    block_count, block_rows, time_rows, trial_rows = blocks.shape
    neuron_rows = block_count * block_rows
    flattened = blocks.reshape(neuron_rows, time_rows, trial_rows)
    rank_size = time_factor.shape[1]
    start_time = lax.psum(
        jnp.dot(time_factor.T, time_factor, preferred_element_type=jnp.float32), "tm"
    )
    start_trial = lax.psum(
        jnp.dot(trial_factor.T, trial_factor, preferred_element_type=jnp.float32), "trial"
    )
    inverse_neuron = normal_inverse(start_time * start_trial)
    kr_tk = khatri_rao(time_factor, trial_factor)
    neuron_total = neuron_rows * lax.axis_size("neuron")
    tensor_piece = flattened
    partial_sums = lax.psum_scatter(
        jnp.einsum("itk,tkr->ir", tensor_piece, kr_tk, preferred_element_type=jnp.float32),
        ("tm", "trial"),
        scatter_dimension=0,
        tiled=True,
    )
    raw_rows = apply_inverse(partial_sums, inverse_neuron)
    gram_sum = lax.psum(raw_gram(raw_rows), ("neuron", "tm", "trial"))
    neuron_own, gram_neuron = rescale(raw_rows, gram_sum, neuron_total)
    neuron_local = lax.all_gather(neuron_own, ("tm", "trial"), axis=0, tiled=True)
    neuron_blocks = neuron_local.reshape(block_count, block_rows, rank_size)
    time_total = time_rows * lax.axis_size("tm")
    inverse_time = normal_inverse(gram_neuron * start_trial)
    own_time = time_rows // (lax.axis_size("neuron") * lax.axis_size("trial"))

    def time_add_block(running, inputs):
        tensor_piece, rows_a = inputs
        kr_ik = khatri_rao(rows_a, trial_factor)
        return (
            running
            + jnp.einsum("itk,ikr->tr", tensor_piece, kr_ik, preferred_element_type=jnp.float32),
            None,
        )

    running, unused = lax.scan(
        time_add_block,
        jnp.zeros((own_time * lax.axis_size(("neuron", "trial")), rank_size), jnp.float32),
        (blocks, neuron_blocks),
    )
    partial_sums = lax.psum_scatter(running, ("neuron", "trial"), scatter_dimension=0, tiled=True)
    raw_rows = apply_inverse(partial_sums, inverse_time)
    gram_sum = lax.psum(raw_gram(raw_rows), ("neuron", "tm", "trial"))
    time_own, gram_time = rescale(raw_rows, gram_sum, time_total)
    time_local = lax.all_gather(time_own, ("neuron", "trial"), axis=0, tiled=True)
    trial_total = trial_rows * lax.axis_size("trial")
    inverse_trial = normal_inverse(gram_neuron * gram_time)
    own_trial = trial_rows // (lax.axis_size("neuron") * lax.axis_size("tm"))

    def trial_add_block(running, inputs):
        tensor_piece, rows_a = inputs
        kr_it = khatri_rao(rows_a, time_local)
        return (
            running
            + jnp.einsum("itk,itr->kr", tensor_piece, kr_it, preferred_element_type=jnp.float32),
            None,
        )

    running, unused = lax.scan(
        trial_add_block,
        jnp.zeros((own_trial * lax.axis_size(("neuron", "tm")), rank_size), jnp.float32),
        (blocks, neuron_blocks),
    )
    partial_sums = lax.psum_scatter(running, ("neuron", "tm"), scatter_dimension=0, tiled=True)
    raw_rows = apply_inverse(partial_sums, inverse_trial)
    squares = lax.psum(jnp.sum(raw_rows * raw_rows, axis=0), ("neuron", "tm", "trial"))
    scales = jnp.sqrt(squares / trial_total + EPSILON)
    trial_own = (raw_rows / scales[None, :]).astype(jnp.bfloat16)
    trial_local = lax.all_gather(trial_own, ("neuron", "tm"), axis=0, tiled=True)
    return (neuron_own, time_local, trial_local)


def solution(mesh):
    return jax.shard_map(
        on_device,
        mesh=mesh,
        in_specs=(
            P("neuron", "tm", "trial"),
            P("neuron", None),
            P("trial"),
            P("tm", None),
            P("trial", None),
        ),
        out_specs=(P(("neuron", "tm", "trial"), None), P("tm", None), P("trial", None)),
        check_vma=False,
    )
```

profile of v0, /device:TPU:0, one launch (start us, length us, event | category | flops | bytes accessed | tf_op | source)
XLA Modules:
  0.0 779.5 jit_solution(2738933545392734299)
XLA Ops:
  8.0 1.8 fusion.88
  10.0 1.8 fusion.87
  14.5 7.2 broadcast_multiply_fusion.1
  21.7 10.2 %fusion.28 = f32[256,256]{1,0:T(8,128)} fusion(f32[128,256]{1,0:T(8,128)S(1)} %convert_element_type.81, f32[128,256]{1,0:T(8,128)S(1)} %convert_element_type.80, bf16[256,128,128]{2,1,0:T(8,128)(2,1)} %broadcast_multiply_fusion.1), kind=kOutput, calls=%fused_computation.38 | convolution fusion | flops 2155872256 | bytes 8912896 | tf_op jit(solution)/shard_map/itk,tkr->ir/dot_general | solution.py:69
  32.6 11.9 %copy.21 = bf16[256,128,128]{1,2,0:T(8,128)(2,1)} copy(bf16[256,128,128]{2,1,0:T(8,128)(2,1)} %param.12) | data formatting | bytes 16777216 | tf_op args[0]
  44.4 13.4 %all-reduce.8.cloned.1.call-done = f32[256,256]{0,1:T(8,128)} async-done(((f32[256,256]{0,1:T(8,128)}), f32[256,256]{0,1:T(8,128)}) %all-reduce.8.cloned.1.call-update) | async-done | bytes 262160 | tf_op jit(solution)/shard_map/psum | solution.py:61
  57.8 20.6 %all-reduce.6.cloned.1.call-done = f32[256,256]{0,1:T(8,128)} async-done(((f32[256,256]{0,1:T(8,128)}), f32[256,256]{0,1:T(8,128)}) %all-reduce.6.cloned.1.call-update) | async-done | bytes 262160 | tf_op jit(solution)/shard_map/psum | solution.py:58
  79.5 2.4 gather_fusion
  83.4 11.7 %cholesky.172 = f32[128,128]{1,0:T(8,128)S(1)} custom-call(f32[128,128]{1,0:T(8,128)S(1)} %cholesky.270), custom_call_target="Cholesky" | custom-call | tf_op jit(solution)/shard_map/jit(cholesky)/cholesky | solution.py:14
  95.1 9.8 %custom-call.29 = f32[1,128,128]{1,2,0:T(8,128)S(1)} custom-call(f32[1,128,128]{2,1,0:T(8,128)S(1)} %get-tuple-element.191), custom_call_target="InvertDiagBlocksLowerTriangular" | custom-call | tf_op jit(solution)/shard_map/jit(cholesky)/cholesky | solution.py:14
  105.4 11.7 %cholesky.189 = f32[128,128]{1,0:T(8,128)S(1)} custom-call(f32[128,128]{1,0:T(8,128)S(1)} %convolution_subtract_fusion.8), custom_call_target="Cholesky" | custom-call | tf_op jit(solution)/shard_map/jit(cholesky)/cholesky | solution.py:14
  119.3 4.0 while.30
  119.9 1.4 bitcast_dynamic-update-slice_fusion.6
  121.9 1.4 bitcast_dynamic-update-slice_fusion.6
  123.3 19.8 %custom-call.30 = f32[2,128,128]{1,2,0:T(8,128)S(1)} custom-call(f32[2,128,128]{2,1,0:T(8,128)S(1)} %get-tuple-element.117), custom_call_target="InvertDiagBlocksLowerTriangular" | custom-call | tf_op jit(solution)/shard_map/jit(_cho_solve)/triangular_solve | solution.py:15
  147.3 7.3 broadcast_multiply_fusion
  154.5 118.6 %all-reduce.10.cloned.1.call-done = f32[256,256]{0,1:T(8,128)} async-done(((f32[256,256]{0,1:T(8,128)}), f32[256,256]{0,1:T(8,128)}) %all-reduce.10.cloned.1.call-update) | async-done | bytes 262160 | tf_op jit(solution)/shard_map/psum | solution.py:75
  273.1 2.6 gather_fusion.1
  276.8 2.4 gather_fusion.2
  280.7 11.7 %cholesky.206 = f32[128,128]{1,0:T(8,128)S(1)} custom-call(f32[128,128]{1,0:T(8,128)S(1)} %cholesky.273), custom_call_target="Cholesky" | custom-call | tf_op jit(solution)/shard_map/jit(cholesky)/cholesky | solution.py:14
  292.5 9.8 %custom-call.31 = f32[1,128,128]{1,2,0:T(8,128)S(1)} custom-call(f32[1,128,128]{2,1,0:T(8,128)S(1)} %get-tuple-element.187), custom_call_target="InvertDiagBlocksLowerTriangular" | custom-call | tf_op jit(solution)/shard_map/jit(cholesky)/cholesky | solution.py:14
  302.8 11.7 %cholesky.223 = f32[128,128]{1,0:T(8,128)S(1)} custom-call(f32[128,128]{1,0:T(8,128)S(1)} %convolution_subtract_fusion.7), custom_call_target="Cholesky" | custom-call | tf_op jit(solution)/shard_map/jit(cholesky)/cholesky | solution.py:14
  317.1 3.8 while.31
  317.7 1.3 bitcast_dynamic-update-slice_fusion.7
  319.6 1.3 bitcast_dynamic-update-slice_fusion.7
  320.9 19.9 %custom-call.32 = f32[2,128,128]{1,2,0:T(8,128)S(1)} custom-call(f32[2,128,128]{2,1,0:T(8,128)S(1)} %get-tuple-element.118), custom_call_target="InvertDiagBlocksLowerTriangular" | custom-call | tf_op jit(solution)/shard_map/jit(_cho_solve)/triangular_solve | solution.py:15
  342.1 23.5 %all_gather.9 = bf16[256,256]{1,0:T(8,128)(2,1)S(1)} all-gather(bf16[32,256]{1,0:T(8,128)(2,1)S(1)} %divide_convert_fusion), channel_id=1, replica_groups=mesh['neuron'=4,'tm'=2,'trial'=4] {'tm','trial'}, dimensions={0}, use_global_device_ids=true | all-gather | bytes 147456 | tf_op jit(solution)/shard_map/all_gather | solution.py:77
  365.6 7.4 while.28
  365.6 3.6 fusion.131
  369.3 3.6 fusion.131
  374.3 74.3 %reduce-scatter.6.cloned.1.call-done = f32[8,256]{1,0:T(8,128)} async-done(((f32[128,256]{1,0:T(8,128)}), f32[8,256]{1,0:T(8,128)}) %reduce-scatter.6.cloned.1.call-update) | async-done | bytes 8208 | tf_op jit(solution)/shard_map/reduce_scatter | solution.py:97
  450.7 124.4 %all-reduce.12.cloned.1.call-done = f32[256,256]{0,1:T(8,128)} async-done(((f32[256,256]{0,1:T(8,128)}), f32[256,256]{0,1:T(8,128)}) %all-reduce.12.cloned.1.call-update) | async-done | bytes 262160 | tf_op jit(solution)/shard_map/psum | solution.py:99
  575.1 2.6 gather_fusion.3
  578.9 2.8 gather_fusion.4
  583.0 11.7 %cholesky.240 = f32[128,128]{1,0:T(8,128)S(1)} custom-call(f32[128,128]{1,0:T(8,128)S(1)} %cholesky.276), custom_call_target="Cholesky" | custom-call | tf_op jit(solution)/shard_map/jit(cholesky)/cholesky | solution.py:14
  594.8 9.8 %custom-call.33 = f32[1,128,128]{1,2,0:T(8,128)S(1)} custom-call(f32[1,128,128]{2,1,0:T(8,128)S(1)} %get-tuple-element.183), custom_call_target="InvertDiagBlocksLowerTriangular" | custom-call | tf_op jit(solution)/shard_map/jit(cholesky)/cholesky | solution.py:14
  605.1 11.7 %cholesky.257 = f32[128,128]{1,0:T(8,128)S(1)} custom-call(f32[128,128]{1,0:T(8,128)S(1)} %convolution_subtract_fusion.6), custom_call_target="Cholesky" | custom-call | tf_op jit(solution)/shard_map/jit(cholesky)/cholesky | solution.py:14
  619.4 3.7 while.32
  620.0 1.3 bitcast_dynamic-update-slice_fusion.8
  621.8 1.3 bitcast_dynamic-update-slice_fusion.8
  623.1 19.8 %custom-call.34 = f32[2,128,128]{1,2,0:T(8,128)S(1)} custom-call(f32[2,128,128]{2,1,0:T(8,128)S(1)} %get-tuple-element.119), custom_call_target="InvertDiagBlocksLowerTriangular" | custom-call | tf_op jit(solution)/shard_map/jit(_cho_solve)/triangular_solve | solution.py:15
  644.3 39.1 %all_gather.10 = bf16[128,256]{1,0:T(8,128)(2,1)S(1)} all-gather(bf16[8,256]{1,0:T(8,128)(2,1)S(1)} %divide_convert_fusion.2), channel_id=1, replica_groups=mesh['neuron'=4,'tm'=2,'trial'=4] {'neuron','trial'}, dimensions={0}, use_global_device_ids=true | all-gather | bytes 69632 | tf_op jit(solution)/shard_map/all_gather | solution.py:101
  683.4 7.2 while.29
  683.4 3.5 fusion.133
  687.0 3.5 fusion.133
  691.8 25.5 %reduce-scatter.8.cloned.1.call-done = f32[16,256]{1,0:T(8,128)} async-done(((f32[128,256]{1,0:T(8,128)}), f32[16,256]{1,0:T(8,128)}) %reduce-scatter.8.cloned.1.call-update) | async-done | bytes 16400 | tf_op jit(solution)/shard_map/reduce_scatter | solution.py:120
  718.3 37.9 %psum.39 = f32[256]{0:T(256)S(1)} all-reduce(f32[256]{0:T(256)S(1)} %get-tuple-element.198), channel_id=1, replica_groups=mesh['neuron'=4,'tm'=2,'trial'=4] {'neuron','tm','trial'}, use_global_device_ids=true, to_apply=%region_19.22 | all-reduce | flops 256 | bytes 2048 | tf_op jit(solution)/shard_map/psum | solution.py:122
  756.2 14.6 %all_gather.11 = bf16[128,256]{1,0:T(8,128)(2,1)S(1)} all-gather(bf16[16,256]{1,0:T(8,128)(2,1)S(1)} %divide_convert_fusion.1), channel_id=1, replica_groups=mesh['neuron'=4,'tm'=2,'trial'=4] {'neuron','tm'}, dimensions={0}, use_global_device_ids=true | all-gather | bytes 73728 | tf_op jit(solution)/shard_map/all_gather | solution.py:125
  (132 shorter events, 31.3 us)
Async XLA Ops:
  8.0 49.8 %all-reduce.8.cloned.1.call-start = ((), (), s32[]{:S(2)}) async-start(), calls=%async_computation.5 | async-start | bytes 524288 | tf_op jit(solution)/shard_map/psum | solution.py:61
  9.9 68.5 %all-reduce.6.cloned.1.call-start = ((), (), s32[]{:S(2)}) async-start(), calls=%async_computation.4 | async-start | bytes 524288 | tf_op jit(solution)/shard_map/psum | solution.py:58
  11.8 133.2 %reduce-scatter.4.cloned.1.call-start = ((), (), s32[]{:S(2)}) async-start(), calls=%async_computation.3 | async-start | bytes 294912 | tf_op jit(solution)/shard_map/reduce_scatter | solution.py:68
  31.9 241.2 %all-reduce.10.cloned.1.call-start = ((), (), s32[]{:S(2)}) async-start(), calls=%async_computation.6 | async-start | bytes 524288 | tf_op jit(solution)/shard_map/psum | solution.py:75
  147.2 301.3 %reduce-scatter.6.cloned.1.call-start = ((), (), s32[]{:S(2)}) async-start(), calls=%async_computation.7 | async-start | bytes 139264 | tf_op jit(solution)/shard_map/reduce_scatter | solution.py:97
  147.3 128.5 %copy-start.2 = (f32[256,256]{0,1:T(8,128)S(1)}, f32[256,256]{0,1:T(8,128)}, u32[]{:S(2)}) copy-start(f32[256,256]{0,1:T(8,128)} %all-reduce.8.cloned.1.call-done) | copy-start | bytes 786436
  154.5 211.0 %copy-start.1 = (bf16[128,256]{1,0:T(8,128)(2,1)S(1)}, bf16[128,256]{1,0:T(8,128)(2,1)}, u32[]{:S(2)}) copy-start(bf16[128,256]{1,0:T(8,128)(2,1)} %param.16) | copy-start | bytes 196612
  275.8 89.8 %copy-start.5 = (bf16[32,256]{1,0:T(8,128)(2,1)}, bf16[32,256]{1,0:T(8,128)(2,1)S(1)}, u32[]{:S(2)}) copy-start(bf16[32,256]{1,0:T(8,128)(2,1)S(1)} %divide_convert_fusion) | copy-start | bytes 49156
  365.6 212.2 %copy-start = (f32[256,256]{0,1:T(8,128)S(1)}, f32[256,256]{0,1:T(8,128)}, u32[]{:S(2)}) copy-start(f32[256,256]{0,1:T(8,128)} %all-reduce.10.cloned.1.call-done) | copy-start | bytes 786436
  373.0 0.6 copy-start.4
  373.7 201.5 %all-reduce.12.cloned.1.call-start = ((), (), s32[]{:S(2)}) async-start(), calls=%async_computation.8 | async-start | bytes 524288 | tf_op jit(solution)/shard_map/psum | solution.py:99
  450.6 266.7 %reduce-scatter.8.cloned.1.call-start = ((), (), s32[]{:S(2)}) async-start(), calls=%async_computation.9 | async-start | bytes 147456 | tf_op jit(solution)/shard_map/reduce_scatter | solution.py:120
  690.5 0.6 copy-start.3
Sparse Core Ops, SparseCore 0:
  12.0 45.7 all-reduce.7
  60.1 18.2 all-reduce.5
  691.3 25.9 reduce-scatter.7
Sparse Core Ops, SparseCore 1:
  32.0 36.4 reduce-scatter.3
  147.3 125.8 all-reduce.9
  373.7 74.7 reduce-scatter.5
  454.1 121.0 all-reduce.11
where the time goes:
time: 785 us; the launch traced here: 780 us
  waiting for transfers between devices  377 us (48%)
  other arithmetic  184 us (23%)
  blocking collectives  115 us (15%)
  matrix products  41.2 us (5%)
  local copies, waits for them, and re-layouts  39.1 us (5%)
  between operations  21.8 us (3%)
    psum x2, waiting for transfers between devices, on_device(): gram_sum = lax.psum(raw_gram(raw_rows), ('neuron', 'tm', 'trial'))  243 us
    another operation x20, other arithmetic, normal_inverse(): lower_factor = jnp.linalg.cholesky(scaled)  103 us
    reduce_scatter x1, waiting for transfers between devices, on_device(): lax.psum_scatter(running, ('neuron', 'trial'), scatter_dimension=0, tiled...  74.3 us
    another operation x7, other arithmetic, normal_inverse(): return jax.scipy.linalg.cho_solve((lower_factor, True), identity)  59.7 us
    all_gather x1, blocking collectives, on_device(): lax.all_gather(time_own, ('neuron', 'trial'), axis=0, tiled=True)  39.1 us
    psum x1, blocking collectives, on_device(): lax.psum(jnp.sum(raw_rows * raw_rows, axis=0), ('neuron', 'tm', 'trial'))  37.9 us
    reduce_scatter x1, waiting for transfers between devices, on_device(): lax.psum_scatter(running, ('neuron', 'tm'), scatter_dimension=0, tiled=True)  25.5 us
    all_gather x1, blocking collectives, on_device(): lax.all_gather(neuron_own, ('tm', 'trial'), axis=0, tiled=True)  23.5 us
  transfers between devices with their start and end apart: 7, of which 6 were waited for; matrix products, arithmetic and copies ran while one was open for 14% of the time, Pallas kernels for 0%

commit v1 on v0

v1 whole, which is shorter than its diff:
```python
import functools

import jax
import jax.numpy as jnp
from jax import lax
from jax.experimental import pallas as pl
from jax.experimental.pallas import tpu as pltpu
from jax.sharding import PartitionSpec as P

RIDGE = 0.1
EPSILON = 1e-06
PANEL = 4
VMEM = pl.BlockSpec(memory_space=pltpu.VMEM)
F32 = jnp.float32
BF16 = jnp.bfloat16
TN = (((0,), (0,)), ((), ()))


def dot_high(left, right):
    return jnp.dot(left, right, precision=lax.Precision.HIGHEST, preferred_element_type=F32)


def gram_high(rows):
    return lax.dot_general(
        rows, rows, TN, precision=lax.Precision.HIGHEST, preferred_element_type=F32
    )


def diagonals(square):
    size = square.shape[0]
    on = lax.broadcasted_iota(jnp.int32, (size, size), 0) == lax.broadcasted_iota(
        jnp.int32, (size, size), 1
    )
    kept = jnp.where(on, square, 0.0)
    return jnp.sum(kept, axis=0, keepdims=True), jnp.sum(kept, axis=1, keepdims=True)


class Group:
    def __init__(self, axes, sizes):
        self.axes = axes
        self.sizes = [sizes[axis] for axis in axes]
        self.count = 1
        for size in self.sizes:
            self.count *= size

    def me(self):
        index = 0
        for axis, size in zip(self.axes, self.sizes):
            index = index * size + lax.axis_index(axis)
        return index

    def where(self, index):
        place = {}
        for axis, size in reversed(list(zip(self.axes, self.sizes))):
            place[axis] = lax.rem(index, size)
            index = index // size
        return place

    def each(self, body):
        if self.count <= 32:
            for step in range(1, self.count):
                body(step)
        else:

            @pl.loop(1, self.count)
            def run(step):
                body(step)

    def greet(self, barrier):
        me = self.me()

        def body(step):
            pl.semaphore_signal(
                barrier,
                inc=1,
                device_id=self.where(lax.rem(me + step, self.count)),
                device_id_type=pl.DeviceIdType.MESH,
            )

        self.each(body)

    def copy(self, step, source, target, sems, incoming):
        me = self.me()
        peer = lax.rem(me + step, self.count)
        origin = lax.rem(me - step + self.count, self.count)
        return pltpu.make_async_remote_copy(
            src_ref=source(peer),
            dst_ref=target(origin if incoming else me),
            send_sem=sems[0].at[step],
            recv_sem=sems[1].at[step],
            device_id=self.where(peer),
            device_id_type=pl.DeviceIdType.MESH,
        )

    def send(self, source, target, sems):
        self.each(lambda step: self.copy(step, source, target, sems, False).start())

    def wait(self, source, target, sems):
        self.each(lambda step: self.copy(step, source, target, sems, True).wait_recv())

    def flush(self, source, target, sems):
        self.each(lambda step: self.copy(step, source, target, sems, False).wait_send())

    def sems(self):
        return [pltpu.SemaphoreType.DMA((self.count,)), pltpu.SemaphoreType.DMA((self.count,))]


def meet(*groups):
    barrier = pltpu.get_barrier_semaphore()
    for group in groups:
        group.greet(barrier)
    pl.semaphore_wait(barrier, sum(group.count - 1 for group in groups))


def call(body, outs, scratch, number, *operands):
    return pl.pallas_call(
        body,
        out_shape=outs,
        in_specs=[VMEM] * len(operands),
        out_specs=[VMEM] * len(outs),
        scratch_shapes=scratch,
        compiler_params=pltpu.CompilerParams(
            collective_id=number, has_side_effects=True, vmem_limit_bytes=32 << 20
        ),
    )(*operands)


def summed(group, own_ref, landed_ref):
    me = group.me()
    landed_ref[me] = own_ref[me]
    if group.count <= 32:
        total = landed_ref[0]
        for index in range(1, group.count):
            total = total + landed_ref[index]
        return total
    return lax.fori_loop(
        1, group.count, lambda index, total: total + landed_ref[index], landed_ref[0]
    )


def start_kernel(by_time, by_trial, time_ref, trial_ref, gram_ref, product_ref, times, trials, ta, tb, ra, rb):
    meet(by_time, by_trial)
    jobs = (
        (by_trial, trial_ref, trials, (ra, rb)),
        (by_time, time_ref, times, (ta, tb)),
    )
    for group, own, landed, sems in jobs:
        group.send(lambda peer: own, lambda index: landed.at[index], sems)
    for group, own, landed, sems in jobs:
        landed[group.me()] = own[...]
        group.wait(lambda peer: own, lambda index: landed.at[index], sems)
    grams = []
    for landed in (times, trials):
        count, rows, rank = landed.shape
        whole = landed[...].reshape(count * rows, rank)
        grams.append(lax.dot_general(whole, whole, TN, preferred_element_type=F32))
    gram_ref[...] = grams[1]
    product_ref[...] = grams[0] * grams[1]
    for group, own, landed, sems in jobs:
        group.flush(lambda peer: own, lambda index: landed.at[index], sems)


def start_products(sizes, time_factor, trial_factor):
    by_time, by_trial = Group(("tm",), sizes), Group(("trial",), sizes)
    rank = time_factor.shape[1]
    square = jax.ShapeDtypeStruct((rank, rank), F32)
    return call(
        functools.partial(start_kernel, by_time, by_trial),
        [square, square],
        [
            pltpu.VMEM((by_time.count, *time_factor.shape), BF16),
            pltpu.VMEM((by_trial.count, *trial_factor.shape), BF16),
            *by_time.sems(),
            *by_trial.sems(),
        ],
        1,
        time_factor,
        trial_factor,
    )


def eliminate(square):
    size = square.shape[0]
    row_id = lax.broadcasted_iota(jnp.int32, (size, size), 0)
    lane_id = lax.broadcasted_iota(jnp.int32, (size, size), 1)
    lane_one = lax.broadcasted_iota(jnp.int32, (1, size), 1)
    for first in range(0, size, PANEL):
        columns = [
            jnp.broadcast_to(square[:, first + j : first + j + 1], (size, size))
            for j in range(PANEL)
        ]
        for j in range(PANEL):
            pivot = first + j
            column = columns[j]
            over = 1.0 / column[pivot : pivot + 1, :]
            row = jnp.where(lane_one == pivot, 1.0, square[pivot : pivot + 1, :]) * over
            square = jnp.where(
                row_id == pivot, row, jnp.where(lane_id == pivot, 0.0, square) - column * row
            )
            for later in range(j + 1, PANEL):
                factor = columns[later][pivot : pivot + 1, :] * over
                columns[later] = jnp.where(
                    row_id == pivot, factor, columns[later] - column * factor
                )
    return square


def inverse_kernel(gram_ref, out_ref):
    size = gram_ref.shape[0]
    half = size // 2
    gram = gram_ref[...]
    across, unused = diagonals(gram)
    mean = jnp.sum(across, axis=1, keepdims=True) / size
    on = lax.broadcasted_iota(jnp.int32, (size, size), 0) == lax.broadcasted_iota(
        jnp.int32, (size, size), 1
    )
    scaled = gram / mean + jnp.where(on, RIDGE, 0.0)
    corner = scaled[:half, half:]
    first = eliminate(scaled[:half, :half])
    carried = dot_high(first, corner)
    rest = scaled[half:, half:] - lax.dot_general(
        corner, carried, TN, precision=lax.Precision.HIGHEST, preferred_element_type=F32
    )
    second = eliminate(rest)
    mixed = dot_high(carried, second)
    out_ref[half:, half:] = second
    out_ref[:half, half:] = -mixed
    out_ref[half:, :half] = -mixed.T
    out_ref[:half, :half] = first + dot_high(mixed, carried.T)


def normal_inverse(gram):
    return pl.pallas_call(
        inverse_kernel,
        out_shape=jax.ShapeDtypeStruct(gram.shape, F32),
        in_specs=[VMEM],
        out_specs=VMEM,
        compiler_params=pltpu.CompilerParams(vmem_limit_bytes=32 << 20),
    )(gram)


def flat(blocks):
    return blocks.reshape(blocks.shape[0] * blocks.shape[1], blocks.shape[2])


def rescaled(raw, gram, total, factor_ref, other, normed_ref, product_ref):
    across, down = diagonals(gram)
    scale = jnp.sqrt(across / total + EPSILON)
    scale_down = jnp.sqrt(down / total + EPSILON)
    factor_ref[...] = (raw / scale).astype(BF16)
    normed = gram / (scale_down * scale)
    normed_ref[...] = normed
    product_ref[...] = normed * other
    return scale


def neuron_kernel(
    plane, depth, total, part, inverse, other, own_ref, local_ref, normed_ref, product_ref,
    landed, raw, grams, slices, gram, sa, sb, ra, rb, za, zb, ga, gb,
):
    meet(plane, depth)
    me = plane.me()
    layer = depth.me()
    size = gram.shape[0] * gram.shape[1]
    sums = (lambda peer: part.at[peer], lambda index: landed.at[index], (sa, sb))
    plane.send(*sums)
    plane.wait(*sums)
    raw[me] = dot_high(summed(plane, part, landed), inverse[...])
    rows = (lambda peer: raw.at[me], lambda index: raw.at[index], (ra, rb))
    plane.send(*rows)
    plane.wait(*rows)
    whole = flat(raw[...])
    grams[...] = gram_high(whole).reshape(grams.shape)
    slices[layer] = grams[me]
    level = (lambda peer: slices.at[layer], lambda index: slices.at[index], (za, zb))
    depth.send(*level)
    depth.wait(*level)
    gram[me] = jnp.sum(slices[...], axis=0)
    spread = (lambda peer: gram.at[me], lambda index: gram.at[index], (ga, gb))
    plane.send(*spread)
    plane.wait(*spread)
    scale = rescaled(
        whole, flat(gram[...]), total, local_ref, other[...], normed_ref, product_ref
    )
    own_ref[...] = (raw[me] / scale).astype(BF16)
    plane.flush(*sums)
    plane.flush(*rows)
    depth.flush(*level)
    plane.flush(*spread)


def finish_neuron(sizes, partial, inverse, other):
    plane, depth = Group(("tm", "trial"), sizes), Group(("neuron",), sizes)
    held, rank = partial.shape
    own = held // plane.count
    piece = rank // plane.count
    square = jax.ShapeDtypeStruct((rank, rank), F32)
    return call(
        functools.partial(neuron_kernel, plane, depth, held * depth.count),
        [
            jax.ShapeDtypeStruct((own, rank), BF16),
            jax.ShapeDtypeStruct((held, rank), BF16),
            square,
            square,
        ],
        [
            pltpu.VMEM((plane.count, own, rank), F32),
            pltpu.VMEM((plane.count, own, rank), F32),
            pltpu.VMEM((plane.count, piece, rank), F32),
            pltpu.VMEM((depth.count, piece, rank), F32),
            pltpu.VMEM((plane.count, piece, rank), F32),
            *plane.sems(),
            *plane.sems(),
            *depth.sems(),
            *plane.sems(),
        ],
        2,
        partial.reshape(plane.count, own, rank),
        inverse,
        other,
    )


def time_kernel(
    ring, pair, total, part, inverse, other, local_ref, normed_ref, product_ref,
    landed, raw, halves, sa, sb, ra, rb, pa, pb,
):
    meet(ring, pair)
    me = ring.me()
    side = pair.me()
    sums = (lambda peer: part.at[peer], lambda index: landed.at[index], (sa, sb))
    ring.send(*sums)
    ring.wait(*sums)
    raw[me] = dot_high(summed(ring, part, landed), inverse[...])
    rows = (lambda peer: raw.at[me], lambda index: raw.at[index], (ra, rb))
    ring.send(*rows)
    ring.wait(*rows)
    mine = flat(raw[...])
    halves[side] = mine
    swap = (lambda peer: halves.at[side], lambda index: halves.at[index], (pa, pb))
    pair.send(*swap)
    pair.wait(*swap)
    gram = gram_high(flat(halves[...]))
    unused = rescaled(mine, gram, total, local_ref, other[...], normed_ref, product_ref)
    ring.flush(*sums)
    ring.flush(*rows)
    pair.flush(*swap)


def finish_time(sizes, partial, inverse, other):
    ring, pair = Group(("neuron", "trial"), sizes), Group(("tm",), sizes)
    held, rank = partial.shape
    own = held // ring.count
    square = jax.ShapeDtypeStruct((rank, rank), F32)
    return call(
        functools.partial(time_kernel, ring, pair, held * pair.count),
        [jax.ShapeDtypeStruct((held, rank), BF16), square, square],
        [
            pltpu.VMEM((ring.count, own, rank), F32),
            pltpu.VMEM((ring.count, own, rank), F32),
            pltpu.VMEM((pair.count, held, rank), F32),
            *ring.sems(),
            *ring.sems(),
            *pair.sems(),
        ],
        3,
        partial.reshape(ring.count, own, rank),
        inverse,
        other,
    )


def trial_kernel(
    ring, everyone, total, part, inverse, local_ref, landed, raw, squares, sa, sb, ra, rb, qa, qb
):
    meet(everyone)
    me = ring.me()
    mine = everyone.me()
    sums = (lambda peer: part.at[peer], lambda index: landed.at[index], (sa, sb))
    ring.send(*sums)
    ring.wait(*sums)
    own = dot_high(summed(ring, part, landed), inverse[...])
    raw[me] = own
    squares[mine] = jnp.sum(own * own, axis=0, keepdims=True)
    rows = (lambda peer: raw.at[me], lambda index: raw.at[index], (ra, rb))
    counts = (lambda peer: squares.at[mine], lambda index: squares.at[index], (qa, qb))
    everyone.send(*counts)
    ring.send(*rows)
    everyone.wait(*counts)
    ring.wait(*rows)
    scale = jnp.sqrt(jnp.sum(squares[...], axis=0) / total + EPSILON)
    local_ref[...] = (flat(raw[...]) / scale).astype(BF16)
    ring.flush(*sums)
    ring.flush(*rows)
    everyone.flush(*counts)


def finish_trial(sizes, partial, inverse):
    ring, everyone = Group(("neuron", "tm"), sizes), Group(("neuron", "tm", "trial"), sizes)
    held, rank = partial.shape
    own = held // ring.count
    return call(
        functools.partial(trial_kernel, ring, everyone, held * sizes["trial"]),
        [jax.ShapeDtypeStruct((held, rank), BF16)],
        [
            pltpu.VMEM((ring.count, own, rank), F32),
            pltpu.VMEM((ring.count, own, rank), F32),
            pltpu.VMEM((everyone.count, 1, rank), F32),
            *ring.sems(),
            *ring.sems(),
            *everyone.sems(),
        ],
        4,
        partial.reshape(ring.count, own, rank),
        inverse,
    )[0]


def khatri_rao(left_rows, right_rows):
    return (
        left_rows.astype(jnp.float32)[:, None, :] * right_rows.astype(jnp.float32)[None, :, :]
    ).astype(jnp.bfloat16)


def mask_tensor(tensor, present_blocks, trial_day):
    day_count = present_blocks.shape[1]
    onehot = (trial_day[:, None] == jnp.arange(day_count, dtype=jnp.int32)[None, :]).astype(
        jnp.float32
    )
    block_mask = jnp.dot(present_blocks.astype(jnp.float32), onehot.T)
    block_count = present_blocks.shape[0]
    shaped = tensor.reshape(
        block_count, tensor.shape[0] // block_count, tensor.shape[1], tensor.shape[2]
    )
    return shaped * block_mask.astype(jnp.bfloat16)[:, None, None, :]


def on_device(sizes, tensor, present_blocks, trial_day, time_factor, trial_factor):
    blocks = mask_tensor(tensor, present_blocks, trial_day)
    block_count, block_rows, time_rows, trial_rows = blocks.shape
    flattened = blocks.reshape(block_count * block_rows, time_rows, trial_rows)
    rank_size = time_factor.shape[1]
    start_trial, product = start_products(sizes, time_factor, trial_factor)
    inverse_neuron = normal_inverse(product)
    kr_tk = khatri_rao(time_factor, trial_factor)
    partial = jnp.einsum("itk,tkr->ir", flattened, kr_tk, preferred_element_type=F32)
    neuron_own, neuron_local, gram_neuron, product = finish_neuron(
        sizes, partial, inverse_neuron, start_trial
    )
    inverse_time = normal_inverse(product)
    neuron_blocks = neuron_local.reshape(block_count, block_rows, rank_size)

    def time_add_block(running, inputs):
        tensor_piece, rows_a = inputs
        kr_ik = khatri_rao(rows_a, trial_factor)
        return (
            running + jnp.einsum("itk,ikr->tr", tensor_piece, kr_ik, preferred_element_type=F32),
            None,
        )

    partial, unused = lax.scan(
        time_add_block, jnp.zeros((time_rows, rank_size), F32), (blocks, neuron_blocks)
    )
    time_local, unused, product = finish_time(sizes, partial, inverse_time, gram_neuron)
    inverse_trial = normal_inverse(product)

    def trial_add_block(running, inputs):
        tensor_piece, rows_a = inputs
        kr_it = khatri_rao(rows_a, time_local)
        return (
            running + jnp.einsum("itk,itr->kr", tensor_piece, kr_it, preferred_element_type=F32),
            None,
        )

    partial, unused = lax.scan(
        trial_add_block, jnp.zeros((trial_rows, rank_size), F32), (blocks, neuron_blocks)
    )
    trial_local = finish_trial(sizes, partial, inverse_trial)
    return (neuron_own, time_local, trial_local)


def solution(mesh):
    sizes = {axis: mesh.shape[axis] for axis in mesh.axis_names}
    return jax.shard_map(
        functools.partial(on_device, sizes),
        mesh=mesh,
        in_specs=(
            P("neuron", "tm", "trial"),
            P("neuron", None),
            P("trial"),
            P("tm", None),
            P("trial", None),
        ),
        out_specs=(P(("neuron", "tm", "trial"), None), P("tm", None), P("trial", None)),
        check_vma=False,
    )
```

time: 785 us -> 158 us (0.20)
  waiting for transfers between devices: 377 us -> 0 us
  other arithmetic: 184 us -> 14.5 us
  blocking collectives: 115 us -> 0 us
  Pallas kernels: 0 us -> 95.4 us
  matrix products: 41.2 us -> 19.7 us
  between operations: 21.8 us -> 0.75 us
  local copies, waits for them, and re-layouts: 39.1 us -> 26.3 us
    psum x4 -> x0, waiting for transfers between devices: 277 us -> none  [the longest x2 243 us: on_device(): gram_sum = lax.psum(raw_gram(raw_rows), ('neuron', 'tm', 'trial'))]
    another operation x27 -> x0, other arithmetic: 163 us -> none  [the longest x20 103 us: normal_inverse(): lower_factor = jnp.linalg.cholesky(scaled)]
    reduce_scatter x3 -> x0, waiting for transfers between devices: 99.8 us -> none  [the longest x1 74.3 us: on_device(): lax.psum_scatter(running, ('neuron', 'trial'), scatter_dimension=0, tiled...]
    pallas_call x0 -> x7, Pallas kernels: none -> 95.4 us  [the longest x4 62.3 us: call(): pl.pallas_call(body, out_shape=outs, in_specs=[VMEM] * len(operands), out...]
    all_gather x3 -> x0, blocking collectives: 77.1 us -> none  [the longest x1 39.1 us: on_device(): lax.all_gather(time_own, ('neuron', 'trial'), axis=0, tiled=True)]
    psum x1 -> x0, blocking collectives: 37.9 us -> none  [on_device(): lax.psum(jnp.sum(raw_rows * raw_rows, axis=0), ('neuron', 'tm', 'trial'))]
    dot_general x12 -> x5, matrix products: 33.3 us -> 18.8 us  [the longest x2 7.08 us: time_add_block(): jnp.einsum('itk,ikr->tr', tensor_piece, kr_ik, preferred_element_type=F32)]
    gather x5 -> x0, local copies, waits for them, and re-layouts: 12.7 us -> none  [the longest x3 7.51 us: normal_inverse(): jnp.diagonal(gram_matrix)]
  transfers between devices with their start and end apart: 7 -> 0, of which waited for: 6 -> 0; matrix products, arithmetic and copies ran while one was open for 14% -> 0% of each run, Pallas kernels for 0% -> 0%
where the time goes in v1:
time: 158 us; the launch traced here: 157 us
  Pallas kernels  95.4 us (60%)
  local copies, waits for them, and re-layouts  26.3 us (17%)
  matrix products  19.7 us (12%)
  other arithmetic  14.5 us (9%)
    pallas_call x4, Pallas kernels, call(): pl.pallas_call(body, out_shape=outs, in_specs=[VMEM] * len(operands), out...  62.3 us
    pallas_call x3, Pallas kernels, normal_inverse(): pl.pallas_call(inverse_kernel, out_shape=jax.ShapeDtypeStruct(gram.shape,...  33.1 us
    mul x2, other arithmetic, mask_tensor(): return shaped * block_mask.astype(jnp.bfloat16)[:, None, None, :]  14.4 us
    unnamed x8, local copies, waits for them, and re-layouts  13.8 us
    dot_general x1, local copies, waits for them, and re-layouts, on_device(): jnp.einsum('itk,tkr->ir', flattened, kr_tk, preferred_element_type=F32)  12.5 us
    dot_general x2, matrix products, time_add_block(): jnp.einsum('itk,ikr->tr', tensor_piece, kr_ik, preferred_element_type=F32)  7.08 us
    dot_general x2, matrix products, trial_add_block(): jnp.einsum('itk,itr->kr', tensor_piece, kr_it, preferred_element_type=F32)  6.95 us
    dot_general x1, matrix products, on_device(): jnp.einsum('itk,tkr->ir', flattened, kr_tk, preferred_element_type=F32)  4.79 us

profile of v1, /device:TPU:0, one launch (start us, length us, event | category | flops | bytes accessed | tf_op | source)
XLA Modules:
  0.0 157.1 jit_solution(8685398382278798105)
XLA Ops:
  0.6 0.9 fusion.32
  1.6 7.2 %broadcast_multiply_fusion.1 = bf16[256,128,128]{2,1,0:T(8,128)(2,1)} fusion(bf16[256,128,128]{2,1,0:T(8,128)(2,1)} %param.9, bf16[256,128]{1,0:T(8,128)(2,1)S(1)} %bitcast.63), kind=kLoop, calls=%fused_computation.26 | loop fusion | flops 4194304 | bytes 16842752 | tf_op jit(solution)/shard_map/mul | solution.py:435
  8.8 0.0 copy-start
  8.8 0.0 copy-start.1
  8.8 12.5 %copy.8 = bf16[8,32,128,128]{3,1,2,0:T(8,128)(2,1)} copy(bf16[8,32,128,128]{2,3,1,0:T(8,128)(2,1)} %bitcast.61) | data formatting | bytes 16777216 | tf_op jit(solution)/shard_map/itk,tkr->ir/dot_general | solution.py:446
  21.2 0.0 copy-done
  21.2 0.0 copy-done.1
  21.3 4.8 %fusion.29.part = f32[8,32,256]{2,1,0:T(8,128)S(1)} fusion(bf16[8,32,128,128]{3,1,2,0:T(8,128)(2,1)} %copy.8, f32[128,256]{1,0:T(8,128)S(1)} %convert_element_type.63, f32[128,256]{1,0:T(8,128)S(1)} %convert_element_type.62), kind=kOutput, calls=%fused_computation.27 | convolution fusion | flops 2155872256 | bytes 8912896 | tf_op jit(solution)/shard_map/itk,tkr->ir/dot_general | solution.py:446
  26.1 8.2 %shard_map.76 = (f32[256,256]{1,0:T(8,128)S(1)}, f32[256,256]{1,0:T(8,128)S(1)}) custom-call(bf16[128,256]{1,0:T(8,128)(2,1)S(1)} %copy-done, bf16[128,256]{1,0:T(8,128)(2,1)S(1)} %copy-done.1), custom_call_target="tpu_custom_call" | custom-call | tf_op jit(solution)/shard_map/pallas_call | solution.py:116
  34.2 11.0 %shard_map.77.inverse = f32[256,256]{1,0:T(8,128)S(1)} custom-call(f32[256,256]{1,0:T(8,128)S(1)} %get-tuple-element.65.gram_ref), custom_call_target="tpu_custom_call" | custom-call | tf_op jit(solution)/shard_map/pallas_call | solution.py:233
  45.3 23.3 %shard_map.78 = (bf16[32,256]{1,0:T(8,128)(2,1)S(1)}, bf16[256,256]{1,0:T(8,128)(2,1)S(1)}, f32[256,256]{1,0:T(8,128)S(1)}, f32[256,256]{1,0:T(8,128)S(1)}) custom-call(f32[8,32,256]{2,1,0:T(8,128)S(1)} %fusion.29.part, f32[256,256]{1,0:T(8,128)S(1)} %shard_map.77.inverse, f32[256,256]{1,0:T(8,128)S(1)} %get-tuple-element.66.other), custom_call_target="tpu_custom_call" | custom-call | tf_op jit(solution)/shard_map/pallas_call | solution.py:116
  68.6 11.9 %copy.9 = bf16[256,128,128]{1,2,0:T(8,128)(2,1)} copy(bf16[256,128,128]{2,1,0:T(8,128)(2,1)} %param.9) | data formatting | bytes 16777216 | tf_op args[0]
  80.5 7.2 %broadcast_multiply_fusion = bf16[2,128,128,128]{2,3,1,0:T(8,128)(2,1)} fusion(bf16[2,128,128,128]{2,3,1,0:T(8,128)(2,1)} %bitcast.60, bf16[2,128]{1,0:T(2,128)(2,1)S(1)} %fusion.32), kind=kLoop, calls=%fused_computation.25 | loop fusion | flops 4194304 | bytes 16777728 | tf_op jit(solution)/shard_map/mul | solution.py:435
  87.8 7.2 %while.22 = (s32[]{:T(128)}, f32[128,256]{1,0:T(8,128)S(1)}, bf16[2,128,128,128]{2,3,1,0:T(8,128)(2,1)}, bf16[2,128,256]{2,1,0:T(8,128)(2,1)S(1)}, bf16[128,256]{1,0:T(8,128)(2,1)S(1)}, /*index=5*/s32[]{:T(128)}, s32[]{:T(128)}) while((s32[]{:T(128)}, f32[128,256]{1,0:T(8,128)S(1)}, bf16[2,128,128,128]{2,3,1,0:T(8,128)(2,1)}, ...), condition=%wide.region_1.2_spmd.clone, body=%wide.region_0.1_spmd.clone.sunk | while | flops 1082261504 | bytes 5112411 | solution.py:461
  87.8 3.5 %fusion.41 = f32[128,256]{1,0:T(8,128)S(1)} fusion(f32[128,256]{1,0:T(8,128)S(1)} %convert_element_type.101, f32[128,256]{1,0:T(8,128)S(1)} %bitcast_convert_fusion.4, bf16[2,128,128,128]{2,3,1,0:T(8,128)(2,1)} %get-tuple-element.214, s32[]{:T(128)} %get-tuple-element.205, f32[128,256]{1,0:T(8,128)S(1)} %get-tuple-element.206, pred[]{:T(512)S(6)} %compare.6), kind=kOutput, calls=%fused_computation.7.clone.1 | convolution fusion | flops 1082195968 | bytes 4719105 | tf_op jit(solution)/shard_map/while/body/eval_jaxpr/itk,ikr->tr/dot_general | solution.py:457
  91.4 3.5 %fusion.41 = f32[128,256]{1,0:T(8,128)S(1)} fusion(f32[128,256]{1,0:T(8,128)S(1)} %convert_element_type.101, f32[128,256]{1,0:T(8,128)S(1)} %bitcast_convert_fusion.4, bf16[2,128,128,128]{2,3,1,0:T(8,128)(2,1)} %get-tuple-element.214, s32[]{:T(128)} %get-tuple-element.205, f32[128,256]{1,0:T(8,128)S(1)} %get-tuple-element.206, pred[]{:T(512)S(6)} %compare.6), kind=kOutput, calls=%fused_computation.7.clone.1 | convolution fusion | flops 1082195968 | bytes 4719105 | tf_op jit(solution)/shard_map/while/body/eval_jaxpr/itk,ikr->tr/dot_general | solution.py:457
  95.0 11.0 %shard_map.79.inverse = f32[256,256]{1,0:T(8,128)S(1)} custom-call(f32[256,256]{1,0:T(8,128)S(1)} %get-tuple-element.70.gram_ref), custom_call_target="tpu_custom_call" | custom-call | tf_op jit(solution)/shard_map/pallas_call | solution.py:233
  106.0 15.8 %shard_map.80 = (bf16[128,256]{1,0:T(8,128)(2,1)S(1)}, f32[256,256]{1,0:T(8,128)}, f32[256,256]{1,0:T(8,128)S(1)}) custom-call(f32[16,8,256]{2,1,0:T(8,128)S(1)} %bitcast.64, f32[256,256]{1,0:T(8,128)S(1)} %shard_map.79.inverse, f32[256,256]{1,0:T(8,128)S(1)} %get-tuple-element.71.other), custom_call_target="tpu_custom_call" | custom-call | tf_op jit(solution)/shard_map/pallas_call | solution.py:116
  121.8 7.3 %while.23 = (s32[]{:T(128)}, f32[128,256]{1,0:T(8,128)S(1)}, bf16[2,128,128,128]{2,3,1,0:T(8,128)(2,1)}, bf16[2,128,256]{2,1,0:T(8,128)(2,1)S(1)}, bf16[128,256]{1,0:T(8,128)(2,1)S(1)}, /*index=5*/s32[]{:T(128)}, s32[]{:T(128)}) while((s32[]{:T(128)}, f32[128,256]{1,0:T(8,128)S(1)}, bf16[2,128,128,128]{2,3,1,0:T(8,128)(2,1)}, ...), condition=%wide.region_3.4_spmd.clone, body=%wide.region_2.3_spmd.clone.sunk | while | flops 1082261504 | bytes 5112411 | solution.py:475
  122.0 3.5 %fusion.43 = f32[128,256]{1,0:T(8,128)S(1)} fusion(f32[128,256]{1,0:T(8,128)S(1)} %convert_element_type.103, f32[128,256]{1,0:T(8,128)S(1)} %bitcast_convert_fusion.5, bf16[2,128,128,128]{2,3,1,0:T(8,128)(2,1)} %get-tuple-element.235, s32[]{:T(128)} %get-tuple-element.226, f32[128,256]{1,0:T(8,128)S(1)} %get-tuple-element.227, pred[]{:T(512)S(6)} %compare.7), kind=kOutput, calls=%fused_computation.17.clone.1 | convolution fusion | flops 1082195968 | bytes 4719105 | tf_op jit(solution)/shard_map/while/body/eval_jaxpr/itk,itr->kr/dot_general | solution.py:471
  125.6 3.5 %fusion.43 = f32[128,256]{1,0:T(8,128)S(1)} fusion(f32[128,256]{1,0:T(8,128)S(1)} %convert_element_type.103, f32[128,256]{1,0:T(8,128)S(1)} %bitcast_convert_fusion.5, bf16[2,128,128,128]{2,3,1,0:T(8,128)(2,1)} %get-tuple-element.235, s32[]{:T(128)} %get-tuple-element.226, f32[128,256]{1,0:T(8,128)S(1)} %get-tuple-element.227, pred[]{:T(512)S(6)} %compare.7), kind=kOutput, calls=%fused_computation.17.clone.1 | convolution fusion | flops 1082195968 | bytes 4719105 | tf_op jit(solution)/shard_map/while/body/eval_jaxpr/itk,itr->kr/dot_general | solution.py:471
  129.1 11.0 %shard_map.81.inverse = f32[256,256]{1,0:T(8,128)S(1)} custom-call(f32[256,256]{1,0:T(8,128)S(1)} %get-tuple-element.74.gram_ref), custom_call_target="tpu_custom_call" | custom-call | tf_op jit(solution)/shard_map/pallas_call | solution.py:233
  140.1 15.1 %shard_map.82 = bf16[128,256]{1,0:T(8,128)(2,1)S(1)} custom-call(f32[8,16,256]{2,1,0:T(8,128)S(1)} %bitcast.65, f32[256,256]{1,0:T(8,128)S(1)} %shard_map.81.inverse), custom_call_target="tpu_custom_call" | custom-call | tf_op jit(solution)/shard_map/pallas_call | solution.py:116
  155.2 0.6 copy.28
  155.8 0.6 copy.29
  156.5 0.6 copy.30
  (13 shorter events, 0.2 us)
Async XLA Ops:
  8.8 12.5 %copy-start = (bf16[128,256]{1,0:T(8,128)(2,1)S(1)}, bf16[128,256]{1,0:T(8,128)(2,1)}, u32[]{:S(2)}) copy-start(bf16[128,256]{1,0:T(8,128)(2,1)} %time_ref.1) | copy-start | bytes 196612
  8.8 12.5 %copy-start.1 = (bf16[128,256]{1,0:T(8,128)(2,1)S(1)}, bf16[128,256]{1,0:T(8,128)(2,1)}, u32[]{:S(2)}) copy-start(bf16[128,256]{1,0:T(8,128)(2,1)} %trial_ref.1) | copy-start | bytes 196612

commit v2 on v1

--- a/solution.py
+++ b/solution.py
@@ -416,65 +416,173 @@
     )[0]
 
 
-def khatri_rao(left_rows, right_rows):
-    return (
-        left_rows.astype(jnp.float32)[:, None, :] * right_rows.astype(jnp.float32)[None, :, :]
-    ).astype(jnp.bfloat16)
-
-
-def mask_tensor(tensor, present_blocks, trial_day):
-    day_count = present_blocks.shape[1]
-    onehot = (trial_day[:, None] == jnp.arange(day_count, dtype=jnp.int32)[None, :]).astype(
-        jnp.float32
-    )
-    block_mask = jnp.dot(present_blocks.astype(jnp.float32), onehot.T)
-    block_count = present_blocks.shape[0]
-    shaped = tensor.reshape(
-        block_count, tensor.shape[0] // block_count, tensor.shape[1], tensor.shape[2]
-    )
-    return shaped * block_mask.astype(jnp.bfloat16)[:, None, None, :]
+def params():
+    return pltpu.CompilerParams(vmem_limit_bytes=40 << 20)
+
+
+def cost(tensor, rank):
+    return pl.CostEstimate(
+        flops=2 * tensor.size * rank, bytes_accessed=2 * tensor.size, transcendentals=0
+    )
+
+
+def neuron_sums_kernel(tensor_ref, mask_ref, time_ref, trial_ref, out_ref):
+    @pl.when(pl.program_id(0) == 0)
+    def clear():
+        out_ref[...] = jnp.zeros_like(out_ref)
+
+    chunk = tensor_ref.shape[1]
+    block_count = mask_ref.shape[0]
+    block_rows = tensor_ref.shape[0] // block_count
+    turned = jnp.swapaxes(tensor_ref[...], 0, 1)
+    times = time_ref[...].astype(F32)
+    trials = trial_ref[...].astype(F32)
+    total = None
+    for first in range(0, chunk, 2):
+        right = jnp.concatenate(
+            [(times[first + j : first + j + 1] * trials).astype(BF16) for j in range(2)], axis=0
+        )
+        left = jnp.concatenate(
+            [
+                jnp.concatenate(
+                    [
+                        turned[first + j, b * block_rows : (b + 1) * block_rows] * mask_ref[b]
+                        for b in range(block_count)
+                    ],
+                    axis=0,
+                )
+                for j in range(2)
+            ],
+            axis=1,
+        )
+        term = jnp.dot(left, right, preferred_element_type=F32)
+        total = term if total is None else total + term
+    out_ref[...] += total
+
+
+def neuron_sums(tensor, mask, time_factor, trial_factor):
+    rows, times, trials = tensor.shape
+    rank = time_factor.shape[1]
+    chunk = 16
+    return pl.pallas_call(
+        neuron_sums_kernel,
+        grid=(times // chunk,),
+        in_specs=[
+            pl.BlockSpec((rows, chunk, trials), lambda g: (0, g, 0)),
+            pl.BlockSpec(mask.shape, lambda g: (0, 0, 0)),
+            pl.BlockSpec((chunk, rank), lambda g: (g, 0)),
+            pl.BlockSpec((trials, rank), lambda g: (0, 0)),
+        ],
+        out_specs=pl.BlockSpec((rows, rank), lambda g: (0, 0)),
+        out_shape=jax.ShapeDtypeStruct((rows, rank), F32),
+        cost_estimate=cost(tensor, rank),
+        compiler_params=params(),
+    )(tensor, mask, time_factor, trial_factor)
+
+
+def time_sums_kernel(tensor_ref, rows_ref, trial_ref, out_ref):
+    @pl.when(pl.program_id(0) == 0)
+    def clear():
+        out_ref[...] = jnp.zeros_like(out_ref)
+
+    chunk = tensor_ref.shape[0]
+    rows = rows_ref[...].astype(F32)
+    trials = trial_ref[0].astype(F32)
+    total = None
+    for first in range(0, chunk, 2):
+        right = jnp.concatenate(
+            [(rows[first + j : first + j + 1] * trials).astype(BF16) for j in range(2)], axis=0
+        )
+        left = jnp.concatenate([tensor_ref[first], tensor_ref[first + 1]], axis=1)
+        term = jnp.dot(left, right, preferred_element_type=F32)
+        total = term if total is None else total + term
+    out_ref[...] += total
+
+
+def time_sums(tensor, masked_trials, neuron_local):
+    rows, times, trials = tensor.shape
+    block_count, unused, rank = masked_trials.shape
+    chunk = 16
+    steps = rows // block_count // chunk
+    return pl.pallas_call(
+        time_sums_kernel,
+        grid=(rows // chunk,),
+        in_specs=[
+            pl.BlockSpec((chunk, times, trials), lambda g: (g, 0, 0)),
+            pl.BlockSpec((chunk, rank), lambda g: (g, 0)),
+            pl.BlockSpec((1, trials, rank), lambda g: (g // steps, 0, 0)),
+        ],
+        out_specs=pl.BlockSpec((times, rank), lambda g: (0, 0)),
+        out_shape=jax.ShapeDtypeStruct((times, rank), F32),
+        cost_estimate=cost(tensor, rank),
+        compiler_params=params(),
+    )(tensor, neuron_local, masked_trials)
+
+
+def trial_sums_kernel(steps, tensor_ref, rows_ref, time_ref, mask_ref, out_ref):
+    @pl.when(pl.program_id(0) == 0)
+    def clear():
+        out_ref[...] = jnp.zeros_like(out_ref)
+
+    chunk = tensor_ref.shape[0]
+    rows = rows_ref[...].astype(F32)
+    times = time_ref[...].astype(F32)
+    mask = mask_ref[0]
+    total = None
+    for first in range(0, chunk, 2):
+        right = jnp.concatenate(
+            [(rows[first + j : first + j + 1] * times).astype(BF16) for j in range(2)], axis=0
+        )
+        left = jnp.concatenate(
+            [tensor_ref[first] * mask, tensor_ref[first + 1] * mask], axis=0
+        )
+        term = lax.dot_general(left, right, TN, preferred_element_type=F32)
+        total = term if total is None else total + term
+    out_ref[...] += total
+
+
+def trial_sums(tensor, mask, neuron_local, time_local):
+    rows, times, trials = tensor.shape
+    rank = time_local.shape[1]
+    chunk = 16
+    steps = rows // mask.shape[0] // chunk
+    return pl.pallas_call(
+        functools.partial(trial_sums_kernel, steps),
+        grid=(rows // chunk,),
+        in_specs=[
+            pl.BlockSpec((chunk, times, trials), lambda g: (g, 0, 0)),
+            pl.BlockSpec((chunk, rank), lambda g: (g, 0)),
+            pl.BlockSpec((times, rank), lambda g: (0, 0)),
+            pl.BlockSpec((1, 1, trials), lambda g: (g // steps, 0, 0)),
+        ],
+        out_specs=pl.BlockSpec((trials, rank), lambda g: (0, 0)),
+        out_shape=jax.ShapeDtypeStruct((trials, rank), F32),
+        cost_estimate=cost(tensor, rank),
+        compiler_params=params(),
+    )(tensor, neuron_local, time_local, mask)
+
+
+def block_mask(present_blocks, trial_day):
+    days = jnp.arange(present_blocks.shape[1], dtype=jnp.int32)
+    onehot = (trial_day[:, None] == days[None, :]).astype(F32)
+    return jnp.dot(present_blocks.astype(F32), onehot.T).astype(BF16)
 
 
 def on_device(sizes, tensor, present_blocks, trial_day, time_factor, trial_factor):
-    blocks = mask_tensor(tensor, present_blocks, trial_day)
-    block_count, block_rows, time_rows, trial_rows = blocks.shape
-    flattened = blocks.reshape(block_count * block_rows, time_rows, trial_rows)
-    rank_size = time_factor.shape[1]
+    flags = block_mask(present_blocks, trial_day)
+    mask = flags[:, None, :]
+    masked_trials = trial_factor[None, :, :] * flags[:, :, None]
     start_trial, product = start_products(sizes, time_factor, trial_factor)
     inverse_neuron = normal_inverse(product)
-    kr_tk = khatri_rao(time_factor, trial_factor)
-    partial = jnp.einsum("itk,tkr->ir", flattened, kr_tk, preferred_element_type=F32)
+    partial = neuron_sums(tensor, mask, time_factor, trial_factor)
     neuron_own, neuron_local, gram_neuron, product = finish_neuron(
         sizes, partial, inverse_neuron, start_trial
     )
     inverse_time = normal_inverse(product)
-    neuron_blocks = neuron_local.reshape(block_count, block_rows, rank_size)
-
-    def time_add_block(running, inputs):
-        tensor_piece, rows_a = inputs
-        kr_ik = khatri_rao(rows_a, trial_factor)
-        return (
-            running + jnp.einsum("itk,ikr->tr", tensor_piece, kr_ik, preferred_element_type=F32),
-            None,
-        )
-
-    partial, unused = lax.scan(
-        time_add_block, jnp.zeros((time_rows, rank_size), F32), (blocks, neuron_blocks)
-    )
+    partial = time_sums(tensor, masked_trials, neuron_local)
     time_local, unused, product = finish_time(sizes, partial, inverse_time, gram_neuron)
     inverse_trial = normal_inverse(product)
-
-    def trial_add_block(running, inputs):
-        tensor_piece, rows_a = inputs
-        kr_it = khatri_rao(rows_a, time_local)
-        return (
-            running + jnp.einsum("itk,itr->kr", tensor_piece, kr_it, preferred_element_type=F32),
-            None,
-        )
-
-    partial, unused = lax.scan(
-        trial_add_block, jnp.zeros((trial_rows, rank_size), F32), (blocks, neuron_blocks)
-    )
+    partial = trial_sums(tensor, mask, neuron_local, time_local)
     trial_local = finish_trial(sizes, partial, inverse_trial)
     return (neuron_own, time_local, trial_local)
 

time: 158 us -> 121 us (0.77)
  local copies, waits for them, and re-layouts: 26.3 us -> 6.95 us
  matrix products: 19.7 us -> 0.9 us
  Pallas kernels: 95.4 us -> 112 us
  other arithmetic: 14.5 us -> 0.1 us
    dot_general x6 -> x1, matrix products: 19.7 us -> 0.9 us  [block_mask(): return jnp.dot(present_blocks.astype(F32), onehot.T).astype(BF16)]
    pallas_call x0 -> x3, Pallas kernels: none -> 16.8 us  [the longest x1 6.36 us: trial_sums(): pl.pallas_call(functools.partial(trial_sums_kernel, steps), grid=(rows //...]
    mul x2 -> x1, other arithmetic: 14.4 us -> 0.1 us  [on_device(): masked_trials = trial_factor[None, :, :] * flags[:, :, None]]
    dot_general x1 -> x0, local copies, waits for them, and re-layouts: 12.5 us -> none  [on_device(): jnp.einsum('itk,tkr->ir', flattened, kr_tk, preferred_element_type=F32)]
    unnamed x8 -> x9, local copies, waits for them, and re-layouts: 13.8 us -> 6.95 us
where the time goes in v2:
time: 121 us
  Pallas kernels  112 us (93%)
  local copies, waits for them, and re-layouts  6.95 us (6%)
    pallas_call x4, Pallas kernels, call(): pl.pallas_call(body, out_shape=outs, in_specs=[VMEM] * len(operands), out...  62.3 us
    pallas_call x3, Pallas kernels, normal_inverse(): pl.pallas_call(inverse_kernel, out_shape=jax.ShapeDtypeStruct(gram.shape,...  33.1 us
    unnamed x9, local copies, waits for them, and re-layouts  6.95 us
    pallas_call x1, Pallas kernels, trial_sums(): pl.pallas_call(functools.partial(trial_sums_kernel, steps), grid=(rows //...  6.36 us
    pallas_call x1, Pallas kernels, time_sums(): pl.pallas_call(time_sums_kernel, grid=(rows // chunk,), in_specs=[pl.Bloc...  5.53 us
    pallas_call x1, Pallas kernels, neuron_sums(): pl.pallas_call(neuron_sums_kernel, grid=(times // chunk,), in_specs=[pl.B...  4.93 us

profile of v2, /device:TPU:0, one launch (start us, length us, event | category | flops | bytes accessed | tf_op | source)
XLA Modules:
  0.0 120.9 jit_solution(5739914253307413087)
XLA Ops:
  0.6 0.9 convolution_convert_fusion
  1.5 0.0 copy-start
  1.5 3.4 %copy-done = bf16[256,128,128]{2,1,0:T(8,128)(2,1)S(1)} copy-done((bf16[256,128,128]{2,1,0:T(8,128)(2,1)S(1)}, bf16[256,128,128]{2,1,0:T(8,128)(2,1)}, u32[]{:S(2)}) %copy-start) | copy-done | bytes 8388632
  4.9 0.0 copy-start.1
  4.9 0.8 copy-done.1
  5.8 0.0 copy-start.2
  5.8 0.8 copy-done.2
  6.6 4.9 %shard_map.76 = f32[256,256]{1,0:T(8,128)S(1)} custom-call(bf16[256,128,128]{2,1,0:T(8,128)(2,1)S(1)} %copy-done, bf16[2,1,128]{2,1,0:T(2,128)(2,1)S(1)} %copy.8.mask_ref, bf16[128,256]{1,0:T(8,128)(2,1)S(1)} %copy-done.2, bf16[128,256]{1,0:T(8,128)(2,1)S(1)} %copy-done.1), custom_call_target="tpu_custom_call" | custom-call | flops 2147483648 | bytes 8388608 | tf_op jit(solution)/shard_map/pallas_call | solution.py:467
  11.6 8.2 %shard_map.77 = (f32[256,256]{1,0:T(8,128)S(1)}, f32[256,256]{1,0:T(8,128)S(1)}) custom-call(bf16[128,256]{1,0:T(8,128)(2,1)S(1)} %copy-done.2, bf16[128,256]{1,0:T(8,128)(2,1)S(1)} %copy-done.1), custom_call_target="tpu_custom_call" | custom-call | tf_op jit(solution)/shard_map/pallas_call | solution.py:116
  19.7 11.0 %shard_map.78.inverse = f32[256,256]{1,0:T(8,128)S(1)} custom-call(f32[256,256]{1,0:T(8,128)S(1)} %get-tuple-element.11.gram_ref), custom_call_target="tpu_custom_call" | custom-call | tf_op jit(solution)/shard_map/pallas_call | solution.py:233
  30.8 23.3 %shard_map.79 = (bf16[32,256]{1,0:T(8,128)(2,1)S(1)}, bf16[256,256]{1,0:T(8,128)(2,1)S(1)}, f32[256,256]{1,0:T(8,128)S(1)}, f32[256,256]{1,0:T(8,128)S(1)}) custom-call(f32[8,32,256]{2,1,0:T(8,128)S(1)} %bitcast.6, f32[256,256]{1,0:T(8,128)S(1)} %shard_map.78.inverse, f32[256,256]{1,0:T(8,128)S(1)} %get-tuple-element.12.other), custom_call_target="tpu_custom_call" | custom-call | tf_op jit(solution)/shard_map/pallas_call | solution.py:116
  54.1 0.1 broadcast_multiply_fusion.trial_ref
  54.2 5.5 %shard_map.80 = f32[128,256]{1,0:T(8,128)S(1)} custom-call(bf16[256,128,128]{2,1,0:T(8,128)(2,1)S(1)} %copy-done, bf16[256,256]{1,0:T(8,128)(2,1)S(1)} %get-tuple-element.14.rows_ref, bf16[2,128,256]{2,1,0:T(8,128)(2,1)S(1)} %broadcast_multiply_fusion.trial_ref), custom_call_target="tpu_custom_call" | custom-call | flops 2147483648 | bytes 8388608 | tf_op jit(solution)/shard_map/pallas_call | solution.py:507
  59.7 11.0 %shard_map.81.inverse = f32[256,256]{1,0:T(8,128)S(1)} custom-call(f32[256,256]{1,0:T(8,128)S(1)} %get-tuple-element.15.gram_ref), custom_call_target="tpu_custom_call" | custom-call | tf_op jit(solution)/shard_map/pallas_call | solution.py:233
  70.8 15.7 %shard_map.82 = (bf16[128,256]{1,0:T(8,128)(2,1)S(1)}, f32[256,256]{1,0:T(8,128)}, f32[256,256]{1,0:T(8,128)S(1)}) custom-call(f32[16,8,256]{2,1,0:T(8,128)S(1)} %bitcast.7, f32[256,256]{1,0:T(8,128)S(1)} %shard_map.81.inverse, f32[256,256]{1,0:T(8,128)S(1)} %get-tuple-element.16.other), custom_call_target="tpu_custom_call" | custom-call | tf_op jit(solution)/shard_map/pallas_call | solution.py:116
  86.5 6.4 %shard_map.83 = f32[128,256]{1,0:T(8,128)S(1)} custom-call(bf16[256,128,128]{2,1,0:T(8,128)(2,1)S(1)} %copy-done, bf16[256,256]{1,0:T(8,128)(2,1)S(1)} %get-tuple-element.14.rows_ref, bf16[128,256]{1,0:T(8,128)(2,1)S(1)} %get-tuple-element.23.time_ref, bf16[2,1,128]{2,1,0:T(2,128)(2,1)S(1)} %copy.8.mask_ref), custom_call_target="tpu_custom_call" | custom-call | flops 2147483648 | bytes 8388608 | tf_op jit(solution)/shard_map/pallas_call | solution.py:549
  92.9 11.0 %shard_map.84.inverse = f32[256,256]{1,0:T(8,128)S(1)} custom-call(f32[256,256]{1,0:T(8,128)S(1)} %get-tuple-element.18.gram_ref), custom_call_target="tpu_custom_call" | custom-call | tf_op jit(solution)/shard_map/pallas_call | solution.py:233
  103.9 15.1 %shard_map.85 = bf16[128,256]{1,0:T(8,128)(2,1)S(1)} custom-call(f32[8,16,256]{2,1,0:T(8,128)S(1)} %bitcast.8, f32[256,256]{1,0:T(8,128)S(1)} %shard_map.84.inverse), custom_call_target="tpu_custom_call" | custom-call | tf_op jit(solution)/shard_map/pallas_call | solution.py:116
  119.0 0.6 copy.13
  119.6 0.6 copy.14
  120.2 0.6 copy.15
  (1 shorter events, 0.0 us)
Async XLA Ops:
  1.5 3.4 %copy-start = (bf16[256,128,128]{2,1,0:T(8,128)(2,1)S(1)}, bf16[256,128,128]{2,1,0:T(8,128)(2,1)}, u32[]{:S(2)}) copy-start(bf16[256,128,128]{2,1,0:T(8,128)(2,1)} %tensor_ref.5) | copy-start | bytes 25165828
  4.9 0.8 copy-start.1
  5.8 0.8 copy-start.2
